TPU v7x, 32 devices: a whole 2x2x4 slice. The times are simulated.
32 devices in a mesh: outer: 2 (over y), inner: 4 (over z), tensor: 4 (over x, core).
Axes of the slice: x: 2, y: 2, z: 4, core: 2. Of those that a mesh axis runs over, the one named last changes fastest.
Arguments:
- queries: bfloat16 [1024, 4096], P(('outer', 'inner'), 'tensor'), may hold values from -12 to 12
- keys: bfloat16 [1024, 512], P(('outer', 'inner'), 'tensor'), may hold values from -12 to 12
- values: bfloat16 [1024, 512], P(('outer', 'inner'), 'tensor'), may hold values from -6 to 6
- ancestors: int32 [8, 4], P(('outer', 'inner')), may hold values from -1 to 7, as said below
- visible_cut: int32 [8, 4], P(('outer', 'inner')), may hold values from 0 to 128, as said below
- positions: int32 [1024], P(('outer', 'inner')), may hold values from 0 to 511, as said below
Outputs:
- attention: bfloat16 [1024, 4096], P(('outer', 'inner', 'tensor'))
Inputs may be any that keep to these rules, and one draw needn't show every extreme that they name: `ancestors`: row i lists block i first, then its parent, the parent's parent and so on to block 0, padded with -1; every parent has a smaller index than its child; some row is full in every draw. `visible_cut`: entry 0 of each row is 128; entry e >= 1 is the offset at which the path leaves block ancestors[i, e], that is the offset of the child of that block on the path; padding entries are 0. Block i's first token sits at its parent's first position plus visible_cut[i, 1] (block 0 starts at 0); positions rise by one inside a block.
All inputs are finite; a program needn't handle non-finite values.
Results may differ from a plain program's by a relative error of at most 0.012.
The roundings to bfloat16 on the way count: a program that leaves them out, or rounds other values in their place, can miss the bound.
Values may be sent and summed in bfloat16 or wider, within the bound.
A program may use at most 64 MiB of HBM per device.

v0:
```python
import math

import jax
import jax.numpy as jnp
from jax import lax
from jax.sharding import PartitionSpec as P

HEAD_SIZE = 128
TREE_BLOCK_SIZE = 128


rope_base = 500000.0
masked_low = -1e30


def apply_rotary(source, positions, head_count):
    token_count = source.shape[0]
    half_dim = HEAD_SIZE // 2
    frequency = jnp.exp(
        jnp.arange(half_dim, dtype=jnp.float32) * (-2.0 / HEAD_SIZE) * math.log(rope_base)
    )
    angles = positions.astype(jnp.float32)[:, None] * frequency[None, :]
    cosines = jnp.cos(angles)[:, None, :]
    sine_vals = jnp.sin(angles)[:, None, :]
    split_heads = source.astype(jnp.float32).reshape(token_count, head_count, HEAD_SIZE)
    front_half = split_heads[..., :half_dim]
    back_half = split_heads[..., half_dim:]
    turned = jnp.concatenate(
        [
            front_half * cosines - back_half * sine_vals,
            back_half * cosines + front_half * sine_vals,
        ],
        axis=-1,
    )
    return turned.reshape(token_count, head_count * HEAD_SIZE).astype(jnp.bfloat16)


def local(queries, keys, values, ancestors, visible_cut, positions):
    row_count = queries.shape[0]
    query_heads = queries.shape[1] // HEAD_SIZE
    kv_heads = keys.shape[1] // HEAD_SIZE
    head_group_width = query_heads // kv_heads
    scale = 1.0 / math.sqrt(HEAD_SIZE)
    rotary_queries = apply_rotary(queries, positions, query_heads)
    rotary_keys = apply_rotary(keys, positions, kv_heads)
    query_grid = rotary_queries.reshape(row_count, kv_heads, head_group_width, HEAD_SIZE)
    first_block = lax.axis_index(("outer", "inner")) * (row_count // TREE_BLOCK_SIZE)
    query_block = first_block + jnp.arange(row_count, dtype=jnp.int32) // TREE_BLOCK_SIZE
    query_inside = jnp.arange(row_count, dtype=jnp.int32) % TREE_BLOCK_SIZE
    key_inside = jnp.arange(TREE_BLOCK_SIZE, dtype=jnp.int32)

    def key_block_step(carried, key_block, val_block, key_id):
        cut_len = jnp.sum(jnp.where(ancestors == key_id, visible_cut, 0), axis=1)
        cut_rows = jnp.repeat(cut_len, TREE_BLOCK_SIZE)
        own_block = query_block == key_id
        visible = (key_inside[None, :] < cut_rows[:, None]) & (
            jnp.logical_not(own_block)[:, None] | (key_inside[None, :] <= query_inside[:, None])
        )

        def compute(state):
            running, total, weighted = state
            scores = (
                jnp.einsum(
                    "tkgd,skd->kgts",
                    query_grid,
                    key_block.reshape(TREE_BLOCK_SIZE, kv_heads, HEAD_SIZE),
                    preferred_element_type=jnp.float32,
                )
                * scale
            )
            scores = jnp.where(visible[None, None], scores, masked_low)
            new_max = jnp.maximum(running, jnp.max(scores, axis=-1))
            exp_terms = jnp.where(visible[None, None], jnp.exp(scores - new_max[..., None]), 0.0)
            rescale = jnp.exp(running - new_max)
            total = total * rescale + jnp.sum(exp_terms, axis=-1)
            weights = exp_terms.astype(jnp.bfloat16)
            update = jnp.einsum(
                "kgts,skd->tkgd",
                weights,
                val_block.reshape(TREE_BLOCK_SIZE, kv_heads, HEAD_SIZE),
                preferred_element_type=jnp.float32,
            )
            weighted = weighted * jnp.transpose(rescale, (2, 0, 1))[..., None] + update
            return (new_max, total, weighted)

        return lax.cond(jnp.any(visible), compute, lambda unchanged: unchanged, carried)

    initial = (
        jnp.full((kv_heads, head_group_width, row_count), masked_low, jnp.float32),
        jnp.zeros((kv_heads, head_group_width, row_count), jnp.float32),
        jnp.zeros((row_count, kv_heads, head_group_width, HEAD_SIZE), jnp.float32),
    )
    key_rows = lax.all_gather(rotary_keys, ("outer", "inner"), axis=0, tiled=True)
    val_rows = lax.all_gather(values, ("outer", "inner"), axis=0, tiled=True)

    def block_step(slot, state):
        key_block = lax.dynamic_slice_in_dim(key_rows, slot * TREE_BLOCK_SIZE, TREE_BLOCK_SIZE, 0)
        val_block = lax.dynamic_slice_in_dim(val_rows, slot * TREE_BLOCK_SIZE, TREE_BLOCK_SIZE, 0)
        return key_block_step(state, key_block, val_block, slot)

    running, total, weighted = lax.fori_loop(
        0, key_rows.shape[0] // TREE_BLOCK_SIZE, block_step, initial
    )
    attended = weighted / jnp.transpose(total, (2, 0, 1))[..., None]
    attended = attended.reshape(row_count, query_heads * HEAD_SIZE).astype(jnp.bfloat16)
    return lax.all_to_all(attended, "tensor", split_axis=0, concat_axis=1, tiled=True)


def solution(mesh):
    placed = (
        P(("outer", "inner"), "tensor"),
        P(("outer", "inner"), "tensor"),
        P(("outer", "inner"), "tensor"),
        P(("outer", "inner"), None),
        P(("outer", "inner"), None),
        P(("outer", "inner")),
    )
    return jax.shard_map(
        local,
        mesh=mesh,
        in_specs=placed,
        out_specs=P(("outer", "inner", "tensor"), None),
        check_vma=False,
    )
```

profile of v0, /device:TPU:4, one launch (start us, length us, event | category | flops | bytes accessed | tf_op | source)
XLA Modules:
  0.0 93.5 jit_solution(4794052715186464259)
XLA Ops:
  0.0 0.6 copy-done.4
  0.7 1.1 %copy.23 = bf16[128,1024]{0,1:T(8,128)(2,1)S(1)} copy(bf16[128,1024]{1,0:T(8,128)(2,1)} %param.10) | data formatting | bytes 524288 | tf_op args[0]
  3.3 27.9 %all-gather = bf16[1024,1,128]{0,2,1:T(8,128)(2,1)S(1)} all-gather(bf16[128,1,128]{0,2,1:T(8,128)(2,1)S(1)} %pad_maximum_fusion.1), channel_id=2, replica_groups=mesh['outer'=2,'inner'=4,'tensor'=4] {'outer','inner'}, dimensions={0}, use_global_device_ids=true | all-gather | bytes 294912 | tf_op jit(solution)/shard_map/all_gather | solution.py:93
  31.3 0.6 copy-done.1
  32.0 27.8 %all_gather.7 = bf16[1024,128]{0,1:T(8,128)(2,1)S(1)} all-gather(bf16[128,128]{0,1:T(8,128)(2,1)S(1)} %copy.24), channel_id=1, replica_groups=mesh['outer'=2,'inner'=4,'tensor'=4] {'outer','inner'}, dimensions={0}, use_global_device_ids=true | all-gather | bytes 294912 | tf_op jit(solution)/shard_map/all_gather | solution.py:94
  59.9 0.6 copy-done.2
  60.5 23.3 %while.19 = (s32[]{:T(128)}, f32[1,8,128]{2,1,0:T(8,128)S(1)}, f32[1,8,128]{2,1,0:T(8,128)S(1)}, f32[128,1,8,128]{0,3,2,1:T(8,128)S(1)}, s32[1,4]{1,0:T(1,128)S(...) while((s32[]{:T(128)}, f32[1,8,128]{2,1,0:T(8,128)S(1)}, ...), condition=%wide.region_7.8_spmd.clone.clone, body=%wide.region_0.7_spmd.clone.clone.sunk | while | flops 68621584 | bytes 3082069 | solution.py:101
  60.5 0.6 fusion.43
  61.1 0.6 compare_not_fusion.2
  61.7 0.7 fusion.44
  63.0 0.8 conditional.4
  63.8 0.6 fusion.43
  65.0 0.7 fusion.44
  66.3 0.8 conditional.4
  67.1 0.6 fusion.43
  68.4 0.7 fusion.44
  69.6 0.8 conditional.4
  70.5 0.6 fusion.43
  71.7 0.7 fusion.44
  73.0 0.6 fusion.43
  73.6 0.6 compare_not_fusion.2
  74.2 0.7 fusion.44
  75.5 0.8 conditional.4
  76.3 0.6 fusion.43
  76.9 0.6 compare_not_fusion.2
  77.5 0.7 fusion.44
  78.8 0.6 fusion.43
  80.0 0.7 fusion.44
  81.3 0.6 fusion.43
  82.6 0.7 fusion.44
  84.2 8.6 %all_to_all.16 = bf16[4,32,1024]{2,1,0:T(8,128)(2,1)S(1)} all-to-all(bf16[4,32,1024]{2,1,0:T(8,128)(2,1)S(1)} %convert_element_type.42), channel_id=1, replica_groups=mesh['outer'=2,'inner'=4,'tensor'=4] {'tensor'}, dimensions={0} | all-to-all | bytes 524288 | tf_op jit(solution)/shard_map/all_to_all | solution.py:106
  92.8 0.7 copy.30
  (67 shorter events, 8.0 us)
Async XLA Ops:
  0.0 0.7 copy-start.4
  2.2 0.8 copy-start
  31.1 0.8 copy-start.1
  59.8 0.7 copy-start.2
  59.8 0.7 copy-start.3
where the time goes:
time: 94 us; the launch traced here: 93.5 us
  blocking collectives  64.2 us (68%)
  other arithmetic  16.4 us (17%)
  local copies, waits for them, and re-layouts  5.2 us (6%)
  loops' own time  5.11 us (5%)
  matrix products  2.46 us (3%)
    all_gather x1, blocking collectives, local(): lax.all_gather(rotary_keys, ('outer', 'inner'), axis=0, tiled=True)  27.9 us
    all_gather x1, blocking collectives, local(): val_rows = lax.all_gather(values, ('outer', 'inner'), axis=0, tiled=True)  27.8 us
    all_to_all x1, blocking collectives, local(): lax.all_to_all(attended, 'tensor', split_axis=0, concat_axis=1, tiled=True)  8.59 us
    and x8, other arithmetic, key_block_step(): (key_inside[None, :] < cut_rows[:, None]) & (jnp.logical_not(own_block)[:...  5.71 us
    reduce_sum x8, other arithmetic, key_block_step(): cut_len = jnp.sum(jnp.where(ancestors == key_id, visible_cut, 0), axis=1)  5.01 us
    another operation x1, loops' own time, local(): lax.fori_loop(0, key_rows.shape[0] // TREE_BLOCK_SIZE, block_step, initial)  4.81 us
    not x8, other arithmetic, key_block_step(): jnp.logical_not(own_block)[:, None]  4.52 us
    unnamed x15, local copies, waits for them, and re-layouts  4.12 us

commit v1 on v0

--- a/solution.py
+++ b/solution.py
@@ -1,8 +1,11 @@
+import functools
 import math
 
 import jax
 import jax.numpy as jnp
 from jax import lax
+from jax.experimental import pallas as pl
+from jax.experimental.pallas import tpu as pltpu
 from jax.sharding import PartitionSpec as P
 
 HEAD_SIZE = 128
@@ -106,6 +109,192 @@
     return lax.all_to_all(attended, "tensor", split_axis=0, concat_axis=1, tiled=True)
 
 
+MESH = pl.DeviceIdType.MESH
+
+
+def fused_kernel(
+    outer_count, inner_count, tensor_count, listed,
+    anc_ref, cut_ref, pos_ref, q_ref, k_ref, v_ref, out_ref,
+    kv, turned, own_scores, staged, kv_send, kv_recv, out_send, out_recv,
+):
+    block_count = outer_count * inner_count
+    width = q_ref.shape[1]
+    heads = width // HEAD_SIZE
+    chunk = TREE_BLOCK_SIZE // tensor_count
+    rows = heads * chunk
+    tensor_me = lax.axis_index("tensor")
+    me = lax.axis_index("outer") * inner_count + lax.axis_index("inner")
+
+    def block_device(j):
+        return {"outer": j // inner_count, "inner": j % inner_count}
+
+    def tensor_peer(step):
+        return lax.rem(tensor_me + step, tensor_count)
+
+    barrier = pltpu.get_barrier_semaphore()
+    for step in range(1, tensor_count):
+        pl.semaphore_signal(barrier, inc=1, device_id={"tensor": tensor_peer(step)}, device_id_type=MESH)
+    for j in range(block_count - 1):
+        @pl.when(j < me)
+        def _():
+            pl.semaphore_signal(barrier, inc=1, device_id=block_device(j), device_id_type=MESH)
+
+    lane = lax.broadcasted_iota(jnp.int32, (TREE_BLOCK_SIZE, HEAD_SIZE), 1)
+    row = lax.broadcasted_iota(jnp.int32, (TREE_BLOCK_SIZE, HEAD_SIZE), 0)
+    half = HEAD_SIZE // 2
+    pair = jnp.where(lane < half, lane, lane - half).astype(jnp.float32)
+    frequency = jnp.exp(pair[:8] * ((-2.0 / HEAD_SIZE) * math.log(rope_base)))
+    near = row[:8].astype(jnp.float32) * frequency
+    near_cos, near_sin = jnp.cos(near), jnp.sin(near)
+    tiles = TREE_BLOCK_SIZE // 8
+    far_rows = (pos_ref[0] + 8 * row[:tiles]).astype(jnp.float32)
+    far = far_rows * frequency[:1]
+    far_cos, far_sin = jnp.cos(far), jnp.sin(far)
+    cos_parts, sin_parts = [], []
+    for tile in range(tiles):
+        fc, fs = far_cos[tile : tile + 1], far_sin[tile : tile + 1]
+        cos_parts.append(fc * near_cos - fs * near_sin)
+        sin_parts.append(fs * near_cos + fc * near_sin)
+    cosines = jnp.concatenate(cos_parts, axis=0)
+    sines = jnp.concatenate(sin_parts, axis=0)
+    sines = jnp.where(lane < half, -sines, sines)
+
+    def rotate(x):
+        x = x.astype(jnp.float32)
+        return (x * cosines + pltpu.roll(x, half, 1) * sines).astype(jnp.bfloat16)
+
+    own_keys = rotate(k_ref[...])
+    kv[me, :TREE_BLOCK_SIZE] = own_keys
+    kv[me, TREE_BLOCK_SIZE:] = v_ref[...]
+
+    pl.semaphore_wait(barrier, tensor_count - 1 + block_count - 1 - me)
+
+    def kv_copy(source, target, sem):
+        return pltpu.make_async_remote_copy(
+            src_ref=kv.at[source], dst_ref=kv.at[source],
+            send_sem=kv_send.at[sem], recv_sem=kv_recv.at[source],
+            device_id=block_device(target), device_id_type=MESH,
+        )
+
+    for j in range(1, block_count):
+        @pl.when(j > me)
+        def _():
+            kv_copy(me, j, j).start()
+
+    for head in range(heads):
+        spun = rotate(q_ref[:, head * HEAD_SIZE : (head + 1) * HEAD_SIZE])
+        for c in range(tensor_count):
+            turned[c, head * chunk : (head + 1) * chunk] = spun[c * chunk : (c + 1) * chunk]
+    row_in = lax.broadcasted_iota(jnp.int32, (rows, TREE_BLOCK_SIZE), 0) % chunk
+    key_in = lax.broadcasted_iota(jnp.int32, (rows, TREE_BLOCK_SIZE), 1)
+    contract_last = (((1,), (1,)), ((), ()))
+    for c in range(tensor_count):
+        s = lax.dot_general(turned[c], own_keys, contract_last, preferred_element_type=jnp.float32)
+        own_scores[c] = jnp.where(key_in <= row_in + c * chunk, s, masked_low)
+
+    for j in range(block_count - 1):
+        @pl.when(j < me)
+        def _():
+            kv_copy(j, j, j).wait_recv()
+
+    key_parts, val_parts, seen = [], [v_ref[...]], []
+    for e in range(1, listed):
+        index = jnp.maximum(anc_ref[0, e], 0)
+        pair_block = kv[index]
+        key_parts.append(pair_block[:TREE_BLOCK_SIZE])
+        val_parts.append(pair_block[TREE_BLOCK_SIZE:])
+        seen.append(key_in < cut_ref[0, e])
+    far_keys = jnp.concatenate(key_parts, axis=0)
+    all_vals = jnp.concatenate(val_parts, axis=0)
+    factor = math.log2(math.e) / math.sqrt(HEAD_SIZE)
+
+    def out_copy(step, column):
+        return pltpu.make_async_remote_copy(
+            src_ref=staged.at[step],
+            dst_ref=out_ref.at[:, pl.ds(pl.multiple_of(column * width, width), width)],
+            send_sem=out_send.at[step], recv_sem=out_recv.at[step],
+            device_id={"tensor": tensor_peer(step)}, device_id_type=MESH,
+        )
+
+    for step in send_order(tensor_count):
+        c = tensor_peer(step)
+        s = lax.dot_general(turned[c], far_keys, contract_last, preferred_element_type=jnp.float32)
+        parts = [own_scores[c]]
+        for e in range(listed - 1):
+            part = s[:, e * TREE_BLOCK_SIZE : (e + 1) * TREE_BLOCK_SIZE]
+            parts.append(jnp.where(seen[e], part, masked_low))
+        top = functools.reduce(jnp.maximum, parts)
+        row_max = jnp.max(top, axis=1, keepdims=True)
+        terms = [jnp.exp2((part - row_max) * factor) for part in parts]
+        total = jnp.sum(functools.reduce(jnp.add, terms), axis=1, keepdims=True)
+        weights = jnp.concatenate([t.astype(jnp.bfloat16) for t in terms], axis=1)
+        summed = jnp.dot(weights, all_vals, preferred_element_type=jnp.float32)
+        result = (summed / total).astype(jnp.bfloat16)
+        for head in range(heads):
+            piece = result[head * chunk : (head + 1) * chunk]
+            if step == 0:
+                column = tensor_me * width + head * HEAD_SIZE
+                out_ref[:, pl.ds(pl.multiple_of(column, HEAD_SIZE), HEAD_SIZE)] = piece
+            else:
+                staged[step, :, head * HEAD_SIZE : (head + 1) * HEAD_SIZE] = piece
+        if step != 0:
+            out_copy(step, tensor_me).start()
+
+    for j in range(1, block_count):
+        @pl.when(j > me)
+        def _():
+            kv_copy(me, j, j).wait_send()
+    for step in range(1, tensor_count):
+        copy = out_copy(step, lax.rem(tensor_me + tensor_count - step, tensor_count))
+        copy.wait_send()
+        copy.wait_recv()
+
+
+def send_order(tensor_count):
+    return list(range(tensor_count - 1, -1, -1))
+
+
+def fused(sizes, queries, keys, values, ancestors, visible_cut, positions):
+    outer_count, inner_count, tensor_count = sizes
+    block_count = outer_count * inner_count
+    width = queries.shape[1]
+    heads = width // HEAD_SIZE
+    chunk = TREE_BLOCK_SIZE // tensor_count
+    listed = ancestors.shape[1]
+    vmem = pl.BlockSpec(memory_space=pltpu.VMEM)
+    smem = pl.BlockSpec(memory_space=pltpu.SMEM)
+    return pl.pallas_call(
+        functools.partial(fused_kernel, outer_count, inner_count, tensor_count, listed),
+        out_shape=jax.ShapeDtypeStruct((chunk, width * tensor_count), jnp.bfloat16),
+        in_specs=[smem, smem, smem, vmem, vmem, vmem],
+        out_specs=vmem,
+        scratch_shapes=[
+            pltpu.VMEM((block_count, 2 * TREE_BLOCK_SIZE, HEAD_SIZE), jnp.bfloat16),
+            pltpu.VMEM((tensor_count, heads * chunk, HEAD_SIZE), jnp.bfloat16),
+            pltpu.VMEM((tensor_count, heads * chunk, TREE_BLOCK_SIZE), jnp.float32),
+            pltpu.VMEM((tensor_count, chunk, width), jnp.bfloat16),
+            pltpu.SemaphoreType.DMA((block_count,)),
+            pltpu.SemaphoreType.DMA((block_count,)),
+            pltpu.SemaphoreType.DMA((tensor_count,)),
+            pltpu.SemaphoreType.DMA((tensor_count,)),
+        ],
+        compiler_params=pltpu.CompilerParams(
+            collective_id=0, has_side_effects=True, vmem_limit_bytes=32 * 1024 * 1024
+        ),
+    )(ancestors, visible_cut, positions, queries, keys, values)
+
+
+def pick(sizes, queries, keys, *rest):
+    small = (
+        queries.shape[0] == TREE_BLOCK_SIZE
+        and keys.shape[1] == HEAD_SIZE
+        and sizes[0] * sizes[1] <= 16
+        and rest[1].shape[1] <= 8
+    )
+    body = functools.partial(fused, sizes) if small else local
+    return body(queries, keys, *rest)
+
+
 def solution(mesh):
     placed = (
         P(("outer", "inner"), "tensor"),
@@ -115,8 +304,9 @@
         P(("outer", "inner"), None),
         P(("outer", "inner")),
     )
+    sizes = tuple(mesh.shape[name] for name in ("outer", "inner", "tensor"))
     return jax.shard_map(
-        local,
+        functools.partial(pick, sizes),
         mesh=mesh,
         in_specs=placed,
         out_specs=P(("outer", "inner", "tensor"), None),

time: 94 us -> 26.7 us (0.28)
  the two profiles are of different devices: /device:TPU:4 before, /device:TPU:28 now
where the time goes in v1:
time: 26.7 us; the launch traced here: 26.4 us
  Pallas kernels  21.2 us (79%)
  local copies, waits for them, and re-layouts  5.13 us (19%)
    pallas_call x1, Pallas kernels, fused(): pl.pallas_call(functools.partial(fused_kernel, outer_count, inner_count,...  21.2 us
    unnamed x13, local copies, waits for them, and re-layouts  5.13 us

profile of v1, /device:TPU:28, one launch (start us, length us, event | category | flops | bytes accessed | tf_op | source)
XLA Modules:
  0.0 26.4 jit_solution(12174616274870583293)
XLA Ops:
  0.0 0.0 copy-start
  0.0 0.9 %copy-done = bf16[128,1024]{1,0:T(8,128)(2,1)S(1)} copy-done((bf16[128,1024]{1,0:T(8,128)(2,1)S(1)}, bf16[128,1024]{1,0:T(8,128)(2,1)}, u32[]{:S(2)}) %copy-start) | copy-done | bytes 262168
  1.0 0.0 copy-start.1
  1.0 0.8 %copy-done.1 = bf16[128,128]{1,0:T(8,128)(2,1)S(1)} copy-done((bf16[128,128]{1,0:T(8,128)(2,1)S(1)}, bf16[128,128]{1,0:T(8,128)(2,1)}, u32[]{:S(2)}) %copy-start.1) | copy-done | bytes 32792
  1.7 0.0 copy-start.2
  1.7 0.8 %copy-done.2 = bf16[128,128]{1,0:T(8,128)(2,1)S(1)} copy-done((bf16[128,128]{1,0:T(8,128)(2,1)S(1)}, bf16[128,128]{1,0:T(8,128)(2,1)}, u32[]{:S(2)}) %copy-start.2) | copy-done | bytes 32792
  2.5 0.0 copy-start.3
  2.5 0.7 %copy-done.3 = s32[1,4]{1,0:T(1,128)S(1)} copy-done((s32[1,4]{1,0:T(1,128)S(1)}, s32[1,4]{1,0:T(1,128)}, u32[]{:S(2)}) %copy-start.3) | copy-done | bytes 40
  3.1 0.0 copy-start.4
  3.1 0.7 %copy-done.4 = s32[1,4]{1,0:T(1,128)S(1)} copy-done((s32[1,4]{1,0:T(1,128)S(1)}, s32[1,4]{1,0:T(1,128)}, u32[]{:S(2)}) %copy-start.4) | copy-done | bytes 40
  3.8 0.0 copy-start.5
  3.8 0.7 %copy-done.5 = s32[128]{0:T(128)S(1)} copy-done((s32[128]{0:T(128)S(1)}, s32[128]{0:T(128)}, u32[]{:S(2)}) %copy-start.5) | copy-done | bytes 536
  4.4 21.2 %shard_map.64 = bf16[32,4096]{1,0:T(8,128)(2,1)S(1)} custom-call(s32[1,4]{1,0:T(1,128)S(1)} %copy-done.3, s32[1,4]{1,0:T(1,128)S(1)} %copy-done.4, s32[128]{0:T(128)S(1)} %copy-done.5, bf16[128,1024]{1,0:T(8,128)(2,1)S(1)} %copy-done, bf16[128,128]{1,0:T(8,128)(2,1)S(1)} %copy-done.1, bf16[128,128]{1,0:T(8,128)(2,1)S(1)} %copy-done.2), custom_call_target="tpu_custom_call" | custom-call | tf_op jit(solution)/shard_map/pallas_call | solution.py:266
  25.6 0.7 %copy.8 = bf16[32,4096]{1,0:T(8,128)(2,1)} copy(bf16[32,4096]{1,0:T(8,128)(2,1)S(1)} %shard_map.64) | data formatting | bytes 524288
Async XLA Ops:
  0.0 0.9 %copy-start = (bf16[128,1024]{1,0:T(8,128)(2,1)S(1)}, bf16[128,1024]{1,0:T(8,128)(2,1)}, u32[]{:S(2)}) copy-start(bf16[128,1024]{1,0:T(8,128)(2,1)} %q_ref.1) | copy-start | bytes 786436
  1.0 0.8 %copy-start.1 = (bf16[128,128]{1,0:T(8,128)(2,1)S(1)}, bf16[128,128]{1,0:T(8,128)(2,1)}, u32[]{:S(2)}) copy-start(bf16[128,128]{1,0:T(8,128)(2,1)} %k_ref.1) | copy-start | bytes 98308
  1.7 0.8 %copy-start.2 = (bf16[128,128]{1,0:T(8,128)(2,1)S(1)}, bf16[128,128]{1,0:T(8,128)(2,1)}, u32[]{:S(2)}) copy-start(bf16[128,128]{1,0:T(8,128)(2,1)} %v_ref.1) | copy-start | bytes 98308
  2.5 0.7 %copy-start.3 = (s32[1,4]{1,0:T(1,128)S(1)}, s32[1,4]{1,0:T(1,128)}, u32[]{:S(2)}) copy-start(s32[1,4]{1,0:T(1,128)} %anc_ref.1) | copy-start | bytes 52
  3.1 0.7 %copy-start.4 = (s32[1,4]{1,0:T(1,128)S(1)}, s32[1,4]{1,0:T(1,128)}, u32[]{:S(2)}) copy-start(s32[1,4]{1,0:T(1,128)} %cut_ref.1) | copy-start | bytes 52
  3.8 0.7 %copy-start.5 = (s32[128]{0:T(128)S(1)}, s32[128]{0:T(128)}, u32[]{:S(2)}) copy-start(s32[128]{0:T(128)} %pos_ref.1) | copy-start | bytes 1540

commit v2 on v1

--- a/solution.py
+++ b/solution.py
@@ -114,8 +114,9 @@
 
 def fused_kernel(
     outer_count, inner_count, tensor_count, listed,
-    anc_ref, cut_ref, pos_ref, q_ref, k_ref, v_ref, out_ref,
-    kv, turned, own_scores, staged, kv_send, kv_recv, out_send, out_recv,
+    anc_hbm, cut_hbm, pos_hbm, q_hbm, k_hbm, v_hbm, out_ref,
+    anc_ref, cut_ref, pos_ref, q_ref, k_ref,
+    kv, turned, own_scores, staged, local_sem, kv_send, kv_pass, kv_recv, out_send, out_recv,
 ):
     block_count = outer_count * inner_count
     width = q_ref.shape[1]
@@ -123,21 +124,46 @@
     chunk = TREE_BLOCK_SIZE // tensor_count
     rows = heads * chunk
     tensor_me = lax.axis_index("tensor")
-    me = lax.axis_index("outer") * inner_count + lax.axis_index("inner")
-
-    def block_device(j):
-        return {"outer": j // inner_count, "inner": j % inner_count}
+    outer_me = lax.axis_index("outer")
+    inner_me = lax.axis_index("inner")
+    me = outer_me * inner_count + inner_me
+    chips = tensor_count // 2
 
     def tensor_peer(step):
-        return lax.rem(tensor_me + step, tensor_count)
+        chip = lax.rem(tensor_me // 2 + step // 2, chips)
+        return chip * 2 + lax.rem(lax.rem(tensor_me, 2) + step % 2, 2)
+
+    def tensor_source(step):
+        chip = lax.rem(tensor_me // 2 + chips - step // 2, chips)
+        return chip * 2 + lax.rem(lax.rem(tensor_me, 2) + step % 2, 2)
+
+    def load(i, source, target):
+        return pltpu.make_async_copy(source, target, local_sem.at[i])
+
+    loads = [
+        load(0, pos_hbm, pos_ref),
+        load(1, k_hbm, k_ref),
+        load(2, v_hbm, kv.at[me, pl.ds(TREE_BLOCK_SIZE, TREE_BLOCK_SIZE)]),
+        load(3, q_hbm, q_ref),
+        load(4, anc_hbm, anc_ref),
+        load(5, cut_hbm, cut_ref),
+    ]
+    for item in loads:
+        item.start()
+
+    def reaches(source_inner, target_inner):
+        return (source_inner != target_inner) & ((outer_me == 0) | (source_inner < target_inner))
 
     barrier = pltpu.get_barrier_semaphore()
     for step in range(1, tensor_count):
         pl.semaphore_signal(barrier, inc=1, device_id={"tensor": tensor_peer(step)}, device_id_type=MESH)
-    for j in range(block_count - 1):
-        @pl.when(j < me)
+    for z in range(inner_count):
+        @pl.when(reaches(z, inner_me))
         def _():
-            pl.semaphore_signal(barrier, inc=1, device_id=block_device(j), device_id_type=MESH)
+            pl.semaphore_signal(barrier, inc=1, device_id={"inner": z}, device_id_type=MESH)
+    @pl.when(outer_me == 1)
+    def _():
+        pl.semaphore_signal(barrier, inc=1, device_id={"outer": 0}, device_id_type=MESH)
 
     lane = lax.broadcasted_iota(jnp.int32, (TREE_BLOCK_SIZE, HEAD_SIZE), 1)
     row = lax.broadcasted_iota(jnp.int32, (TREE_BLOCK_SIZE, HEAD_SIZE), 0)
@@ -147,6 +173,7 @@
     near = row[:8].astype(jnp.float32) * frequency
     near_cos, near_sin = jnp.cos(near), jnp.sin(near)
     tiles = TREE_BLOCK_SIZE // 8
+    loads[0].wait()
     far_rows = (pos_ref[0] + 8 * row[:tiles]).astype(jnp.float32)
     far = far_rows * frequency[:1]
     far_cos, far_sin = jnp.cos(far), jnp.sin(far)
@@ -163,28 +190,51 @@
         x = x.astype(jnp.float32)
         return (x * cosines + pltpu.roll(x, half, 1) * sines).astype(jnp.bfloat16)
 
+    loads[1].wait()
     own_keys = rotate(k_ref[...])
     kv[me, :TREE_BLOCK_SIZE] = own_keys
-    kv[me, TREE_BLOCK_SIZE:] = v_ref[...]
-
-    pl.semaphore_wait(barrier, tensor_count - 1 + block_count - 1 - me)
-
-    def kv_copy(source, target, sem):
+    loads[2].wait()
+
+    sends = jnp.where(outer_me == 0, inner_count, inner_count - 1 - inner_me)
+    pl.semaphore_wait(barrier, tensor_count - 1 + sends)
+
+    def kv_copy(block, z):
         return pltpu.make_async_remote_copy(
-            src_ref=kv.at[source], dst_ref=kv.at[source],
-            send_sem=kv_send.at[sem], recv_sem=kv_recv.at[source],
-            device_id=block_device(target), device_id_type=MESH,
+            src_ref=kv.at[block], dst_ref=kv.at[block],
+            send_sem=kv_send.at[z], recv_sem=kv_recv.at[block],
+            device_id={"inner": z}, device_id_type=MESH,
         )
 
-    for j in range(1, block_count):
-        @pl.when(j > me)
-        def _():
-            kv_copy(me, j, j).start()
-
+    def kv_forward(block):
+        return pltpu.make_async_remote_copy(
+            src_ref=kv.at[block], dst_ref=kv.at[block],
+            send_sem=kv_pass.at[block], recv_sem=kv_recv.at[block],
+            device_id={"outer": 1}, device_id_type=MESH,
+        )
+
+    @pl.when(outer_me == 0)
+    def _():
+        kv_forward(inner_me).start()
+    for distance in range(inner_count - 1, 0, -1):
+        for z in (inner_me - distance, inner_me + distance):
+            @pl.when((z >= 0) & (z < inner_count) & reaches(inner_me, z))
+            def _():
+                kv_copy(me, z).start()
+
+    def pass_on(distance):
+        for z in (inner_me - distance, inner_me + distance):
+            @pl.when((outer_me == 0) & (z >= 0) & (z < inner_count))
+            def _():
+                kv_copy(z, z).wait_recv()
+                kv_forward(z).start()
+
+    loads[3].wait()
     for head in range(heads):
         spun = rotate(q_ref[:, head * HEAD_SIZE : (head + 1) * HEAD_SIZE])
         for c in range(tensor_count):
             turned[c, head * chunk : (head + 1) * chunk] = spun[c * chunk : (c + 1) * chunk]
+    for distance in range(1, inner_count):
+        pass_on(distance)
     row_in = lax.broadcasted_iota(jnp.int32, (rows, TREE_BLOCK_SIZE), 0) % chunk
     key_in = lax.broadcasted_iota(jnp.int32, (rows, TREE_BLOCK_SIZE), 1)
     contract_last = (((1,), (1,)), ((), ()))
@@ -193,11 +243,13 @@
         own_scores[c] = jnp.where(key_in <= row_in + c * chunk, s, masked_low)
 
     for j in range(block_count - 1):
-        @pl.when(j < me)
+        @pl.when((outer_me == 1) & (j < me))
         def _():
-            kv_copy(j, j, j).wait_recv()
-
-    key_parts, val_parts, seen = [], [v_ref[...]], []
+            kv_copy(j, inner_me).wait_recv()
+    loads[4].wait()
+    loads[5].wait()
+
+    key_parts, val_parts, seen = [], [kv[me][TREE_BLOCK_SIZE:]], []
     for e in range(1, listed):
         index = jnp.maximum(anc_ref[0, e], 0)
         pair_block = kv[index]
@@ -240,12 +292,15 @@
         if step != 0:
             out_copy(step, tensor_me).start()
 
-    for j in range(1, block_count):
-        @pl.when(j > me)
+    for z in range(inner_count):
+        @pl.when(reaches(inner_me, z))
         def _():
-            kv_copy(me, j, j).wait_send()
+            kv_copy(me, z).wait_send()
+        @pl.when(outer_me == 0)
+        def _():
+            kv_forward(z).wait_send()
     for step in range(1, tensor_count):
-        copy = out_copy(step, lax.rem(tensor_me + tensor_count - step, tensor_count))
+        copy = out_copy(step, tensor_source(step))
         copy.wait_send()
         copy.wait_recv()
 
@@ -261,25 +316,31 @@
     heads = width // HEAD_SIZE
     chunk = TREE_BLOCK_SIZE // tensor_count
     listed = ancestors.shape[1]
-    vmem = pl.BlockSpec(memory_space=pltpu.VMEM)
-    smem = pl.BlockSpec(memory_space=pltpu.SMEM)
+    hbm = pl.BlockSpec(memory_space=pltpu.HBM)
     return pl.pallas_call(
         functools.partial(fused_kernel, outer_count, inner_count, tensor_count, listed),
         out_shape=jax.ShapeDtypeStruct((chunk, width * tensor_count), jnp.bfloat16),
-        in_specs=[smem, smem, smem, vmem, vmem, vmem],
-        out_specs=vmem,
+        in_specs=[hbm] * 6,
+        out_specs=pl.BlockSpec(memory_space=pltpu.VMEM),
         scratch_shapes=[
+            pltpu.SMEM(ancestors.shape, jnp.int32),
+            pltpu.SMEM(visible_cut.shape, jnp.int32),
+            pltpu.SMEM(positions.shape, jnp.int32),
+            pltpu.VMEM(queries.shape, jnp.bfloat16),
+            pltpu.VMEM(keys.shape, jnp.bfloat16),
             pltpu.VMEM((block_count, 2 * TREE_BLOCK_SIZE, HEAD_SIZE), jnp.bfloat16),
             pltpu.VMEM((tensor_count, heads * chunk, HEAD_SIZE), jnp.bfloat16),
             pltpu.VMEM((tensor_count, heads * chunk, TREE_BLOCK_SIZE), jnp.float32),
             pltpu.VMEM((tensor_count, chunk, width), jnp.bfloat16),
-            pltpu.SemaphoreType.DMA((block_count,)),
+            pltpu.SemaphoreType.DMA((6,)),
+            pltpu.SemaphoreType.DMA((inner_count,)),
+            pltpu.SemaphoreType.DMA((inner_count,)),
             pltpu.SemaphoreType.DMA((block_count,)),
             pltpu.SemaphoreType.DMA((tensor_count,)),
             pltpu.SemaphoreType.DMA((tensor_count,)),
         ],
         compiler_params=pltpu.CompilerParams(
-            collective_id=0, has_side_effects=True, vmem_limit_bytes=32 * 1024 * 1024
+            collective_id=0, has_side_effects=True, vmem_limit_bytes=64 * 1024 * 1024
         ),
     )(ancestors, visible_cut, positions, queries, keys, values)
 
@@ -288,7 +349,9 @@
     small = (
         queries.shape[0] == TREE_BLOCK_SIZE
         and keys.shape[1] == HEAD_SIZE
-        and sizes[0] * sizes[1] <= 16
+        and sizes[0] == 2
+        and sizes[1] <= 8
+        and sizes[2] % 2 == 0
         and rest[1].shape[1] <= 8
     )
     body = functools.partial(fused, sizes) if small else local

time: 26.7 us -> 21.3 us (0.80)
  the two profiles are of different devices: /device:TPU:28 before, /device:TPU:20 now
where the time goes in v2:
time: 21.3 us; the launch traced here: 21.2 us
  Pallas kernels  19.5 us (92%)
  local copies, waits for them, and re-layouts  1.67 us (8%)
    pallas_call x1, Pallas kernels, fused(): pl.pallas_call(functools.partial(fused_kernel, outer_count, inner_count,...  19.5 us
    unnamed x1, local copies, waits for them, and re-layouts  1.67 us

profile of v2, /device:TPU:20, one launch (start us, length us, event | category | flops | bytes accessed | tf_op | source)
XLA Modules:
  0.0 21.2 jit_solution(13379466279462781865)
XLA Ops:
  0.0 19.5 %shard_map.64 = bf16[32,4096]{1,0:T(8,128)(2,1)} custom-call(s32[1,4]{1,0:T(1,128)} %anc_hbm.1, s32[1,4]{1,0:T(1,128)} %cut_hbm.1, s32[128]{0:T(128)} %pos_hbm.1, bf16[128,1024]{1,0:T(8,128)(2,1)} %q_hbm.1, bf16[128,128]{1,0:T(8,128)(2,1)} %k_hbm.1, bf16[128,128]{1,0:T(8,128)(2,1)} %v_hbm.1), custom_call_target="tpu_custom_call" | custom-call | tf_op jit(solution)/shard_map/pallas_call | solution.py:320
  19.5 1.7 %copy.8 = bf16[32,4096]{1,0:T(8,128)(2,1)} copy(bf16[32,4096]{1,0:T(8,128)(2,1)} %shard_map.64) | data formatting | bytes 524288

commit v3 on v2

--- a/solution.py
+++ b/solution.py
@@ -152,7 +152,7 @@
         item.start()
 
     def reaches(source_inner, target_inner):
-        return (source_inner != target_inner) & ((outer_me == 0) | (source_inner < target_inner))
+        return source_inner < target_inner
 
     barrier = pltpu.get_barrier_semaphore()
     for step in range(1, tensor_count):
@@ -161,9 +161,10 @@
         @pl.when(reaches(z, inner_me))
         def _():
             pl.semaphore_signal(barrier, inc=1, device_id={"inner": z}, device_id_type=MESH)
-    @pl.when(outer_me == 1)
-    def _():
-        pl.semaphore_signal(barrier, inc=1, device_id={"outer": 0}, device_id_type=MESH)
+    for z in range(inner_count):
+        @pl.when((outer_me == 1) & (z >= inner_me))
+        def _():
+            pl.semaphore_signal(barrier, inc=1, device_id={"outer": 0, "inner": z}, device_id_type=MESH)
 
     lane = lax.broadcasted_iota(jnp.int32, (TREE_BLOCK_SIZE, HEAD_SIZE), 1)
     row = lax.broadcasted_iota(jnp.int32, (TREE_BLOCK_SIZE, HEAD_SIZE), 0)
@@ -205,6 +206,13 @@
             device_id={"inner": z}, device_id_type=MESH,
         )
 
+    def kv_down(z):
+        return pltpu.make_async_remote_copy(
+            src_ref=kv.at[me], dst_ref=kv.at[me],
+            send_sem=kv_send.at[z], recv_sem=kv_recv.at[me],
+            device_id={"outer": 1, "inner": z}, device_id_type=MESH,
+        )
+
     def kv_forward(block):
         return pltpu.make_async_remote_copy(
             src_ref=kv.at[block], dst_ref=kv.at[block],
@@ -215,18 +223,20 @@
     @pl.when(outer_me == 0)
     def _():
         kv_forward(inner_me).start()
-    for distance in range(inner_count - 1, 0, -1):
-        for z in (inner_me - distance, inner_me + distance):
-            @pl.when((z >= 0) & (z < inner_count) & reaches(inner_me, z))
-            def _():
-                kv_copy(me, z).start()
+    for distance in range(1, inner_count):
+        @pl.when(inner_me + distance < inner_count)
+        def _():
+            kv_copy(me, inner_me + distance).start()
+        @pl.when((outer_me == 0) & (inner_me - distance >= 0))
+        def _():
+            kv_down(inner_me - distance).start()
 
     def pass_on(distance):
-        for z in (inner_me - distance, inner_me + distance):
-            @pl.when((outer_me == 0) & (z >= 0) & (z < inner_count))
-            def _():
-                kv_copy(z, z).wait_recv()
-                kv_forward(z).start()
+        z = inner_me - distance
+        @pl.when((outer_me == 0) & (z >= 0))
+        def _():
+            kv_copy(z, z).wait_recv()
+            kv_forward(z).start()
 
     loads[3].wait()
     for head in range(heads):
@@ -296,7 +306,10 @@
         @pl.when(reaches(inner_me, z))
         def _():
             kv_copy(me, z).wait_send()
-        @pl.when(outer_me == 0)
+        @pl.when((outer_me == 0) & (z < inner_me))
+        def _():
+            kv_down(z).wait_send()
+        @pl.when((outer_me == 0) & (z <= inner_me))
         def _():
             kv_forward(z).wait_send()
     for step in range(1, tensor_count):

time: 21.3 us -> 20.1 us (0.944)
  the two profiles are of different devices: /device:TPU:20 before, /device:TPU:28 now
where the time goes in v3:
time: 20.1 us; the launch traced here: 20 us
  Pallas kernels  18.3 us (91%)
  local copies, waits for them, and re-layouts  1.67 us (8%)
    pallas_call x1, Pallas kernels, fused(): pl.pallas_call(functools.partial(fused_kernel, outer_count, inner_count,...  18.3 us
    unnamed x1, local copies, waits for them, and re-layouts  1.67 us

profile of v3, /device:TPU:28, one launch (start us, length us, event | category | flops | bytes accessed | tf_op | source)
XLA Modules:
  0.0 20.0 jit_solution(13426977984145201538)
XLA Ops:
  0.0 18.3 %shard_map.64 = bf16[32,4096]{1,0:T(8,128)(2,1)} custom-call(s32[1,4]{1,0:T(1,128)} %anc_hbm.1, s32[1,4]{1,0:T(1,128)} %cut_hbm.1, s32[128]{0:T(128)} %pos_hbm.1, bf16[128,1024]{1,0:T(8,128)(2,1)} %q_hbm.1, bf16[128,128]{1,0:T(8,128)(2,1)} %k_hbm.1, bf16[128,128]{1,0:T(8,128)(2,1)} %v_hbm.1), custom_call_target="tpu_custom_call" | custom-call | tf_op jit(solution)/shard_map/pallas_call | solution.py:333
  18.3 1.7 %copy.8 = bf16[32,4096]{1,0:T(8,128)(2,1)} copy(bf16[32,4096]{1,0:T(8,128)(2,1)} %shard_map.64) | data formatting | bytes 524288

commit v4 on v3

--- a/solution.py
+++ b/solution.py
@@ -152,7 +152,8 @@
         item.start()
 
     def reaches(source_inner, target_inner):
-        return source_inner < target_inner
+        relayed = (lax.rem(source_inner, 2) == 1) & (target_inner - source_inner == 2)
+        return (source_inner < target_inner) & jnp.logical_not(relayed)
 
     barrier = pltpu.get_barrier_semaphore()
     for step in range(1, tensor_count):
@@ -196,8 +197,11 @@
     kv[me, :TREE_BLOCK_SIZE] = own_keys
     loads[2].wait()
 
-    sends = jnp.where(outer_me == 0, inner_count, inner_count - 1 - inner_me)
-    pl.semaphore_wait(barrier, tensor_count - 1 + sends)
+    sends = inner_count - 1 - inner_me + jnp.where(outer_me == 0, inner_me + 1, 0)
+    inner_odd = lax.rem(inner_me, 2) == 1
+    relays = jnp.logical_not(inner_odd) & (inner_me >= 2) & (inner_me + 1 < inner_count)
+    skips = jnp.where(inner_odd & (inner_me + 2 < inner_count), 1, 0)
+    pl.semaphore_wait(barrier, tensor_count - 1 + sends - skips)
 
     def kv_copy(block, z):
         return pltpu.make_async_remote_copy(
@@ -224,19 +228,35 @@
     def _():
         kv_forward(inner_me).start()
     for distance in range(1, inner_count):
-        @pl.when(inner_me + distance < inner_count)
+        @pl.when((inner_me + distance < inner_count) & reaches(inner_me, inner_me + distance))
         def _():
             kv_copy(me, inner_me + distance).start()
         @pl.when((outer_me == 0) & (inner_me - distance >= 0))
         def _():
             kv_down(inner_me - distance).start()
+
+    def kv_relay():
+        return pltpu.make_async_remote_copy(
+            src_ref=kv.at[me - 1], dst_ref=kv.at[me - 1],
+            send_sem=kv_pass.at[inner_me + 1], recv_sem=kv_recv.at[me - 1],
+            device_id={"inner": inner_me + 1}, device_id_type=MESH,
+        )
 
     def pass_on(distance):
         z = inner_me - distance
         @pl.when((outer_me == 0) & (z >= 0))
         def _():
             kv_copy(z, z).wait_recv()
+            if distance == 1:
+                @pl.when(relays)
+                def _():
+                    kv_relay().start()
             kv_forward(z).start()
+        if distance == 1:
+            @pl.when((outer_me == 1) & relays)
+            def _():
+                kv_relay().wait_recv()
+                kv_relay().start()
 
     loads[3].wait()
     for head in range(heads):
@@ -253,7 +273,7 @@
         own_scores[c] = jnp.where(key_in <= row_in + c * chunk, s, masked_low)
 
     for j in range(block_count - 1):
-        @pl.when((outer_me == 1) & (j < me))
+        @pl.when((outer_me == 1) & (j < me) & jnp.logical_not(relays & (j == me - 1)))
         def _():
             kv_copy(j, inner_me).wait_recv()
     loads[4].wait()
@@ -312,6 +332,9 @@
         @pl.when((outer_me == 0) & (z <= inner_me))
         def _():
             kv_forward(z).wait_send()
+    @pl.when(relays)
+    def _():
+        kv_relay().wait_send()
     for step in range(1, tensor_count):
         copy = out_copy(step, tensor_source(step))
         copy.wait_send()

time: 20.1 us -> 18.9 us (0.940)
  Pallas kernels: 18.3 us -> 17.1 us
    pallas_call x1, Pallas kernels: 18.3 us -> 17.1 us  [fused(): pl.pallas_call(functools.partial(fused_kernel, outer_count, inner_count,...]
where the time goes in v4:
time: 18.9 us; the launch traced here: 18.8 us
  Pallas kernels  17.1 us (90%)
  local copies, waits for them, and re-layouts  1.67 us (9%)
    pallas_call x1, Pallas kernels, fused(): pl.pallas_call(functools.partial(fused_kernel, outer_count, inner_count,...  17.1 us
    unnamed x1, local copies, waits for them, and re-layouts  1.67 us

profile of v4, /device:TPU:28, one launch (start us, length us, event | category | flops | bytes accessed | tf_op | source)
XLA Modules:
  0.0 18.8 jit_solution(5238734252536696660)
XLA Ops:
  0.0 17.1 %shard_map.64 = bf16[32,4096]{1,0:T(8,128)(2,1)} custom-call(s32[1,4]{1,0:T(1,128)} %anc_hbm.1, s32[1,4]{1,0:T(1,128)} %cut_hbm.1, s32[128]{0:T(128)} %pos_hbm.1, bf16[128,1024]{1,0:T(8,128)(2,1)} %q_hbm.1, bf16[128,128]{1,0:T(8,128)(2,1)} %k_hbm.1, bf16[128,128]{1,0:T(8,128)(2,1)} %v_hbm.1), custom_call_target="tpu_custom_call" | custom-call | tf_op jit(solution)/shard_map/pallas_call | solution.py:356
  17.1 1.7 %copy.8 = bf16[32,4096]{1,0:T(8,128)(2,1)} copy(bf16[32,4096]{1,0:T(8,128)(2,1)} %shard_map.64) | data formatting | bytes 524288

commit v5 on v4

--- a/solution.py
+++ b/solution.py
@@ -110,6 +110,23 @@
 
 
 MESH = pl.DeviceIdType.MESH
+
+
+class Halves:
+    def __init__(self, half):
+        self.parts = [half(0), half(1)]
+
+    def start(self):
+        for part in self.parts:
+            part.start()
+
+    def wait_send(self):
+        for part in self.parts:
+            part.wait_send()
+
+    def wait_recv(self):
+        for part in self.parts:
+            part.wait_recv()
 
 
 def fused_kernel(
@@ -204,25 +221,44 @@
     pl.semaphore_wait(barrier, tensor_count - 1 + sends - skips)
 
     def kv_copy(block, z):
-        return pltpu.make_async_remote_copy(
-            src_ref=kv.at[block], dst_ref=kv.at[block],
-            send_sem=kv_send.at[z], recv_sem=kv_recv.at[block],
-            device_id={"inner": z}, device_id_type=MESH,
-        )
+        def half(h):
+            part = kv.at[block, pl.ds(h * TREE_BLOCK_SIZE, TREE_BLOCK_SIZE)]
+            return pltpu.make_async_remote_copy(
+                src_ref=part, dst_ref=part,
+                send_sem=kv_send.at[h, z], recv_sem=kv_recv.at[h, block],
+                device_id={"inner": z}, device_id_type=MESH,
+            )
+        return Halves(half)
 
     def kv_down(z):
-        return pltpu.make_async_remote_copy(
-            src_ref=kv.at[me], dst_ref=kv.at[me],
-            send_sem=kv_send.at[z], recv_sem=kv_recv.at[me],
-            device_id={"outer": 1, "inner": z}, device_id_type=MESH,
-        )
+        def half(h):
+            part = kv.at[me, pl.ds(h * TREE_BLOCK_SIZE, TREE_BLOCK_SIZE)]
+            return pltpu.make_async_remote_copy(
+                src_ref=part, dst_ref=part,
+                send_sem=kv_send.at[h, z], recv_sem=kv_recv.at[h, me],
+                device_id={"outer": 1, "inner": z}, device_id_type=MESH,
+            )
+        return Halves(half)
 
     def kv_forward(block):
-        return pltpu.make_async_remote_copy(
-            src_ref=kv.at[block], dst_ref=kv.at[block],
-            send_sem=kv_pass.at[block], recv_sem=kv_recv.at[block],
-            device_id={"outer": 1}, device_id_type=MESH,
-        )
+        def half(h):
+            part = kv.at[block, pl.ds(h * TREE_BLOCK_SIZE, TREE_BLOCK_SIZE)]
+            return pltpu.make_async_remote_copy(
+                src_ref=part, dst_ref=part,
+                send_sem=kv_pass.at[h, block], recv_sem=kv_recv.at[h, block],
+                device_id={"outer": 1}, device_id_type=MESH,
+            )
+        return Halves(half)
+
+    def kv_relay():
+        def half(h):
+            part = kv.at[me - 1, pl.ds(h * TREE_BLOCK_SIZE, TREE_BLOCK_SIZE)]
+            return pltpu.make_async_remote_copy(
+                src_ref=part, dst_ref=part,
+                send_sem=kv_pass.at[h, inner_me + 1], recv_sem=kv_recv.at[h, me - 1],
+                device_id={"inner": inner_me + 1}, device_id_type=MESH,
+            )
+        return Halves(half)
 
     @pl.when(outer_me == 0)
     def _():
@@ -235,28 +271,23 @@
         def _():
             kv_down(inner_me - distance).start()
 
-    def kv_relay():
-        return pltpu.make_async_remote_copy(
-            src_ref=kv.at[me - 1], dst_ref=kv.at[me - 1],
-            send_sem=kv_pass.at[inner_me + 1], recv_sem=kv_recv.at[me - 1],
-            device_id={"inner": inner_me + 1}, device_id_type=MESH,
-        )
-
     def pass_on(distance):
         z = inner_me - distance
         @pl.when((outer_me == 0) & (z >= 0))
         def _():
-            kv_copy(z, z).wait_recv()
-            if distance == 1:
-                @pl.when(relays)
-                def _():
-                    kv_relay().start()
-            kv_forward(z).start()
+            for h in range(2):
+                kv_copy(z, z).parts[h].wait_recv()
+                if distance == 1:
+                    @pl.when(relays)
+                    def _():
+                        kv_relay().parts[h].start()
+                kv_forward(z).parts[h].start()
         if distance == 1:
             @pl.when((outer_me == 1) & relays)
             def _():
-                kv_relay().wait_recv()
-                kv_relay().start()
+                for h in range(2):
+                    kv_relay().parts[h].wait_recv()
+                    kv_relay().parts[h].start()
 
     loads[3].wait()
     for head in range(heads):
@@ -369,9 +400,9 @@
             pltpu.VMEM((tensor_count, heads * chunk, TREE_BLOCK_SIZE), jnp.float32),
             pltpu.VMEM((tensor_count, chunk, width), jnp.bfloat16),
             pltpu.SemaphoreType.DMA((6,)),
-            pltpu.SemaphoreType.DMA((inner_count,)),
-            pltpu.SemaphoreType.DMA((inner_count,)),
-            pltpu.SemaphoreType.DMA((block_count,)),
+            pltpu.SemaphoreType.DMA((2, inner_count)),
+            pltpu.SemaphoreType.DMA((2, inner_count)),
+            pltpu.SemaphoreType.DMA((2, block_count)),
             pltpu.SemaphoreType.DMA((tensor_count,)),
             pltpu.SemaphoreType.DMA((tensor_count,)),
         ],

time: 18.9 us -> 18.7 us (0.989)
  Pallas kernels: 17.1 us -> 16.9 us
    pallas_call x1, Pallas kernels: 17.1 us -> 16.9 us  [fused(): pl.pallas_call(functools.partial(fused_kernel, outer_count, inner_count,...]
where the time goes in v5:
time: 18.7 us; the launch traced here: 18.6 us
  Pallas kernels  16.9 us (90%)
  local copies, waits for them, and re-layouts  1.67 us (9%)
    pallas_call x1, Pallas kernels, fused(): pl.pallas_call(functools.partial(fused_kernel, outer_count, inner_count,...  16.9 us
    unnamed x1, local copies, waits for them, and re-layouts  1.67 us

profile of v5, /device:TPU:28, one launch (start us, length us, event | category | flops | bytes accessed | tf_op | source)
XLA Modules:
  0.0 18.6 jit_solution(9378023851234808784)
XLA Ops:
  0.0 16.9 %shard_map.64 = bf16[32,4096]{1,0:T(8,128)(2,1)} custom-call(s32[1,4]{1,0:T(1,128)} %anc_hbm.1, s32[1,4]{1,0:T(1,128)} %cut_hbm.1, s32[128]{0:T(128)} %pos_hbm.1, bf16[128,1024]{1,0:T(8,128)(2,1)} %q_hbm.1, bf16[128,128]{1,0:T(8,128)(2,1)} %k_hbm.1, bf16[128,128]{1,0:T(8,128)(2,1)} %v_hbm.1), custom_call_target="tpu_custom_call" | custom-call | tf_op jit(solution)/shard_map/pallas_call | solution.py:387
  16.9 1.7 %copy.8 = bf16[32,4096]{1,0:T(8,128)(2,1)} copy(bf16[32,4096]{1,0:T(8,128)(2,1)} %shard_map.64) | data formatting | bytes 524288

commit v6 on v5

--- a/solution.py
+++ b/solution.py
@@ -289,12 +289,13 @@
                     kv_relay().parts[h].wait_recv()
                     kv_relay().parts[h].start()
 
+    pass_on(1)
     loads[3].wait()
     for head in range(heads):
         spun = rotate(q_ref[:, head * HEAD_SIZE : (head + 1) * HEAD_SIZE])
         for c in range(tensor_count):
             turned[c, head * chunk : (head + 1) * chunk] = spun[c * chunk : (c + 1) * chunk]
-    for distance in range(1, inner_count):
+    for distance in range(2, inner_count):
         pass_on(distance)
     row_in = lax.broadcasted_iota(jnp.int32, (rows, TREE_BLOCK_SIZE), 0) % chunk
     key_in = lax.broadcasted_iota(jnp.int32, (rows, TREE_BLOCK_SIZE), 1)

time: 18.7 us -> 18.7 us (level)
  no operation moved by 1% of the time
where the time goes in v6:
time: 18.7 us; the launch traced here: 18.6 us
  Pallas kernels  16.9 us (90%)
  local copies, waits for them, and re-layouts  1.67 us (9%)
    pallas_call x1, Pallas kernels, fused(): pl.pallas_call(functools.partial(fused_kernel, outer_count, inner_count,...  16.9 us
    unnamed x1, local copies, waits for them, and re-layouts  1.67 us

profile of v6, /device:TPU:28, one launch (start us, length us, event | category | flops | bytes accessed | tf_op | source)
XLA Modules:
  0.0 18.6 jit_solution(3897047406406609246)
XLA Ops:
  0.0 16.9 %shard_map.64 = bf16[32,4096]{1,0:T(8,128)(2,1)} custom-call(s32[1,4]{1,0:T(1,128)} %anc_hbm.1, s32[1,4]{1,0:T(1,128)} %cut_hbm.1, s32[128]{0:T(128)} %pos_hbm.1, bf16[128,1024]{1,0:T(8,128)(2,1)} %q_hbm.1, bf16[128,128]{1,0:T(8,128)(2,1)} %k_hbm.1, bf16[128,128]{1,0:T(8,128)(2,1)} %v_hbm.1), custom_call_target="tpu_custom_call" | custom-call | tf_op jit(solution)/shard_map/pallas_call | solution.py:388
  16.9 1.7 %copy.8 = bf16[32,4096]{1,0:T(8,128)(2,1)} copy(bf16[32,4096]{1,0:T(8,128)(2,1)} %shard_map.64) | data formatting | bytes 524288
